TPU v7x, 512 devices: a whole 4x4x16 slice. The times are simulated.
512 devices in a mesh: dp: 16 (over z), ep: 32 (over x, y, core).
Axes of the slice: x: 4, y: 4, z: 16, core: 2. Of those that a mesh axis runs over, the one named last changes fastest.
Arguments:
- tokens: bfloat16 [16, 4096, 2880], P('dp', 'ep'), may hold values from -6 to 6
- expert_ids: int32 [16, 4096, 4], P('dp', 'ep'), may hold values from 0 to 127, as said below
- slot_pos: int32 [16, 4096, 4], P('dp', 'ep'), may hold values from -1 to 4, as said below
- smooth: float32 [4, 2880], replicated, may hold values from 0.25 to 4
- smoothed_weight: bfloat16 [2880, 2, 11520], P('dp', None, 'ep'), may hold values from -0.109375 to 0.109375
- act_grad: bfloat16 [16, 160, 11520], P('dp', None, 'ep'), may hold values from -1.5 to 1.5
Outputs:
- token_grad: bfloat16 [16, 4096, 2880], P('dp', 'ep')
- weight_grad: float32 [2880, 2, 11520], P('dp', None, 'ep')
Inputs may be any that keep to these rules, and one draw needn't show every extreme that they name: `expert_ids`: each token names 4 different experts, at most one of them below 4. `slot_pos`: -1 where the named expert is 4 or above; otherwise the slot of the token in that expert's buffer for the 128 tokens of its block, distinct within the buffer. In every draw one expert below 4 has a full buffer from every block.
All inputs are finite; a program needn't handle non-finite values.
Results may differ from a plain program's by a relative error of at most 0.017.
Values may be sent and summed in bfloat16 or wider, within the bound.
A program may use at most 64 MiB of HBM per device.

v0:
```python
import functools

import jax
import jax.numpy as jnp
from jax import lax
from jax.experimental import pallas as pl
from jax.experimental.pallas import tpu as pltpu
from jax.sharding import PartitionSpec as P

MESH = pl.DeviceIdType.MESH
F32 = jnp.float32
BF16 = jnp.bfloat16
ALPHA = 1.702
Z = 16
E = 32
SHARE = 8
SLOT = 5
ROWS = 160
D = 2880
KC = 180
KP = 184
CH = 1024
HID = 360
HP = 384
WIDE = 1024
BLK = 16
THIRDS = ((0, 1024), (1024, 1024), (2048, 832))
C4, C5, USED = 720, 900, 1020
SUBS = ((0, 368), (368, 352), (720, 144), (864, 160))
BACK = ((0, 352), (352, 368), (720, 144), (864, 160))
N = len(SUBS)
FAR = (0, 2)


def mm(a, b):
    return jnp.dot(a, b, preferred_element_type=F32)


def mm_nt(a, b):
    return lax.dot_general(a, b, (((1,), (1,)), ((), ())), preferred_element_type=F32)


def mm_tn(a, b):
    return lax.dot_general(a, b, (((0,), (0,)), ((), ())), preferred_element_type=F32)


def kernel(
    w_ref, tok_ref, ids_ref, pos_ref, smooth_ref, act_ref,
    dw_ref, dtok_ref,
    tok_vm, tok_sem, wbuf, tsend, trecv, rows32, d32, sct, scy, scz, fcol, acc, gall, cbuf, rsend, rrecv, bthird, psend, precv, actc,
    ag_ss, ag_rs, rs_ss, rs_rs, t_ss, t_rs, p_ss, p_rs,
):
    z = lax.axis_index("dp")
    me = lax.axis_index("ep")
    right, left = lax.rem(z + 1, Z), lax.rem(z + Z - 1, Z)
    group = me // SHARE
    sides = (right, left)

    barrier = pltpu.get_barrier_semaphore()
    for side in sides:
        pl.semaphore_signal(barrier, inc=1, device_id={"dp": side}, device_id_type=MESH)

    @pl.loop(1, E)
    def _(k):
        pl.semaphore_signal(
            barrier, inc=1, device_id={"ep": lax.rem(me + k, E)}, device_id_type=MESH
        )

    tok_load = pltpu.make_async_copy(tok_ref, tok_vm, tok_sem)
    tok_load.start()

    def lanes(rows, low, high):
        lane = lax.broadcasted_iota(jnp.int32, (rows, 128), 1)
        return (lane >= low) & (lane < high)

    def roll(x, shift):
        return pltpu.roll(x, shift, 1)

    def own_chunk():
        for u in range(2):
            for half in range(2):
                at = half * 2 * KC + u * KC
                piece = w_ref[u, :, half * 128 : half * 128 + 128].astype(F32)
                cbuf[0, at : at + KC] = piece[0:KC]
        gate = w_ref[0, :, 256:384].astype(F32)
        up = w_ref[1, :, 256:384].astype(F32)
        cbuf[0, C4:C5] = jnp.where(lanes(KP, 0, 104), gate, roll(up, 104))[0:KC]
        for at in range(2):
            cbuf[at, USED:CH] = jnp.zeros((CH - USED, 128), F32)
        cbuf[0, C5:USED] = jnp.where(lanes(120, 0, 80), roll(up[0:120], 104), 0.0)
        low = up[120:180]
        cbuf[0, C5 : C5 + 60] = cbuf[0, C5 : C5 + 60] + jnp.where(
            lanes(60, 80, 128), roll(low, 56), 0.0
        )
        cbuf[0, C5 + 60 : USED] = cbuf[0, C5 + 60 : USED] + jnp.where(
            lanes(60, 80, 112), roll(low, 8), 0.0
        )
        wbuf[z] = cbuf[0].astype(BF16)

    own_chunk()
    pl.semaphore_wait(barrier, E + 1)

    def far(way, sub):
        return (sub in FAR) == (way == 0)

    def ag_copy(s, way, sub, owner):
        first, count = SUBS[sub]
        part = wbuf.at[owner, pl.ds(first, count)]
        return pltpu.make_async_remote_copy(
            src_ref=part, dst_ref=part,
            send_sem=ag_ss.at[way, s, sub], recv_sem=ag_rs.at[way, s, sub],
            device_id={"dp": sides[way]}, device_id_type=MESH,
        )

    def ag_send(s, way, sub):
        owner = lax.rem(z + Z - s, Z) if way == 0 else lax.rem(z + s, Z)
        return ag_copy(s, way, sub, owner)

    def ag_recv(s, way, sub):
        owner = lax.rem(z + Z - 1 - s, Z) if way == 0 else lax.rem(z + 1 + s, Z)
        return ag_copy(s, way, sub, owner)

    def ag_sent(s):
        for sub in range(N):
            for way in range(2):
                if s < 7 or far(way, sub):
                    ag_send(s, way, sub).wait_send()

    for sub in range(N):
        for way in range(2):
            ag_send(0, way, sub).start()

    def match_rows(count, shift):
        row = lax.broadcasted_iota(jnp.int32, (count, 128), 0)
        g = row >> shift
        j = row & (BLK - 1)
        slot = (j * 11) >> 5
        third = j - 3 * slot
        hit = jnp.zeros((count, 128), jnp.bool_)
        for k in range(4):
            hit = hit | ((ids_ref[k : k + 1, :] == g) & (pos_ref[k : k + 1, :] == slot))
        return [
            jnp.where(hit & (third == t), 1.0, 0.0).astype(BF16) for t in range(3)
        ]

    tok_load.wait()
    sel = match_rows(4 * BLK, 4)
    for t, (first, count) in enumerate(THIRDS):
        rows = mm_nt(sel[t], tok_vm[first : first + count, :])
        if t == 0:
            rows32[...] = rows
        else:
            rows32[:, 0:count] = rows32[:, 0:count] + rows
    for g in range(4):
        tsend[g] = rows32[g * BLK : (g + 1) * BLK, :].astype(BF16)

    def t_copy(peer, block, slot_at, peer_sem):
        return pltpu.make_async_remote_copy(
            src_ref=tsend.at[block], dst_ref=trecv.at[slot_at],
            send_sem=t_ss.at[peer], recv_sem=t_rs.at[peer_sem],
            device_id={"ep": peer}, device_id_type=MESH,
        )

    @pl.loop(1, E)
    def _(k):
        peer = lax.rem(me + k, E)
        t_copy(peer, peer // SHARE, me, me).start()

    trecv[me] = tsend[group]

    def place_rows(t, tall, first=0, count=E * BLK):
        shape = (count, ROWS) if tall else (ROWS, count)
        wide = lax.broadcasted_iota(jnp.int32, shape, 0 if tall else 1) + first
        r = lax.broadcasted_iota(jnp.int32, shape, 1 if tall else 0)
        s = (r * 205) >> 10
        return jnp.where(wide == s * BLK + (r - SLOT * s) * 3 + t, 1.0, 0.0).astype(BF16)

    def t_sent():
        @pl.loop(1, E)
        def _(k):
            peer = lax.rem(me + k, E)
            t_copy(peer, peer // SHARE, me, me).wait_send()

    def t_wait():
        @pl.loop(1, E)
        def _(k):
            peer = lax.rem(me + E - k, E)
            t_copy(peer, 0, peer, peer).wait_recv()

    def factors():
        row = smooth_ref[pl.ds(group, 1), :]
        for first, count in THIRDS:
            piece = jnp.broadcast_to(row[:, first : first + count], (8, count))
            fcol[first : first + count, :] = piece.T
        acc[...] = jnp.zeros_like(acc)
        actc[...] = jnp.zeros_like(actc)
        actc[:, 0:104] = act_ref[:, 256:360].astype(F32)

    def dispatch(t):
        first, count = THIRDS[t]
        wide = trecv[...].reshape(E * BLK, WIDE)
        rows = mm(place_rows(t, False), wide[:, 0:count])
        factor = smooth_ref[pl.ds(group, 1), first : first + count]
        scaled = (rows / factor).astype(BF16).astype(F32)
        d32[first : first + count, :] = scaled.T
        if t == 2:
            d32[D : D + 64, :] = jnp.zeros((64, ROWS), F32)

    def chunks(low, high):
        for o in range(low, high):
            at = KC * o
            row = lax.broadcasted_iota(jnp.int32, (KP, ROWS), 0)
            sct[o] = jnp.where(row < KC, d32[at : at + KP, :], 0.0).astype(BF16)
            row = lax.broadcasted_iota(jnp.int32, (120, ROWS), 0)
            scy[o] = jnp.where(row < 60, d32[at + 120 : at + 240, :], 0.0).astype(BF16)
            scz[o] = jnp.where(row >= 60, d32[at + 60 : at + 180, :], 0.0).astype(BF16)

    def forward(o, part):
        if part < 2:
            first = 2 * KC * part
            pair = jnp.concatenate(
                [wbuf[o, first : first + KC], wbuf[o, first + KC : first + 2 * KC]], axis=1
            )
            at = 256 * part
            acc[:, at : at + 256] = acc[:, at : at + 256] + mm_tn(sct[o, 0:KC], pair)
        else:
            block = wbuf[o, C5:USED]
            acc[:, 512:640] = acc[:, 512:640] + mm_tn(sct[o, 0:KC], wbuf[o, C4:C5])
            acc[:, 640:768] = acc[:, 640:768] + mm_tn(sct[o, 0:120], block)
            acc[:, 768:896] = acc[:, 768:896] + mm_tn(scy[o], block)
            acc[:, 896:1024] = acc[:, 896:1024] + mm_tn(scz[o], block)

    def forward_at(*steps):
        for d in steps:
            for part in range(3):
                forward(lax.rem(z + Z + d, Z), part)

    def forward_pair(d, part):
        forward(lax.rem(z + Z + d, Z), part)
        forward(lax.rem(z + Z - d, Z), part)

    ag_tasks = {
        (1, 0): factors,
        (3, 1): lambda: (t_wait(), dispatch(0)),
        (3, 2): lambda: dispatch(1),
        (3, 3): lambda: dispatch(2),
        (4, 0): lambda: chunks(0, 4),
        (4, 1): lambda: chunks(4, 8),
        (4, 2): lambda: chunks(8, 12),
        (4, 3): lambda: chunks(12, 16),
        (5, 0): lambda: forward_at(0, 1),
        (5, 1): lambda: forward_at(-1, 2),
        (5, 2): lambda: forward_at(-2, 3),
        (5, 3): lambda: forward_at(-3, 4),
        (6, 0): lambda: forward_at(-4, 5),
        (6, 1): lambda: forward_at(-5),
        (6, 2): t_sent,
        (6, 3): lambda: forward_at(-6),
        (7, 0): lambda: (forward_pair(7, 0), forward(lax.rem(z + 6, Z), 0)),
        (7, 1): lambda: (forward_pair(7, 1), forward(lax.rem(z + 6, Z), 1)),
        (7, 2): lambda: forward(lax.rem(z + 6, Z), 2),
        (7, 3): lambda: forward_pair(7, 2),
    }
    for s in range(1, 8):
        for sub in range(N):
            for way in range(2):
                ag_recv(s - 1, way, sub).wait_recv()
                if s < 7 or far(way, sub):
                    ag_send(s, way, sub).start()
            ag_tasks.get((s, sub), lambda: None)()
        if s > 1:
            ag_sent(s - 2)

    def gradients(gate, up, c):
        q = 1.0 / (1.0 + jnp.exp(-ALPHA * gate))
        gg = c * (up + 1.0) * q * (1.0 + ALPHA * gate * (1.0 - q))
        return gg, c * gate * q

    def activate(part):
        at = 256 * part
        if part < 2:
            c = act_ref[:, 128 * part : 128 * part + 128].astype(F32)
            gg, gu = gradients(acc[:, at : at + 128], acc[:, at + 128 : at + 256], c)
            gall[:, at : at + 128] = gg.astype(BF16)
            gall[:, at + 128 : at + 256] = gu.astype(BF16)
            return
        gate = acc[:, 512:640]
        up = jnp.where(lanes(ROWS, 0, 24), roll(gate, 24), 0.0)
        up = jnp.where(lanes(ROWS, 24, 104), roll(acc[:, 640:768], 24), up)
        up = up + jnp.where(lanes(ROWS, 24, 72), roll(acc[:, 768:896], 72), 0.0)
        up = up + jnp.where(lanes(ROWS, 72, 104), roll(acc[:, 896:1024], 120), 0.0)
        gg, gu = gradients(gate, up, actc[...])
        turned = roll(gu, 104)
        gall[:, 512:640] = jnp.where(lanes(ROWS, 0, 104), gg, turned).astype(BF16)
        gall[:, 640:768] = jnp.where(lanes(ROWS, 0, 80), turned, 0.0).astype(BF16)
        gall[:, 768:896] = jnp.where(lanes(ROWS, 80, 128), roll(gu, 56), 0.0).astype(BF16)
        gall[:, 896:1024] = jnp.where(lanes(ROWS, 80, 112), roll(gu, 8), 0.0).astype(BF16)

    def term(o, part, at):
        if part < 2:
            pair = mm(sct[o], gall[:, 256 * part : 256 * part + 256])
            first = 2 * KC * part
            cbuf[at, first : first + KC] = pair[0:KC, 0:128]
            cbuf[at, first + KC : first + 2 * KC] = pair[0:KC, 128:256]
        else:
            cbuf[at, C4:C5] = mm(sct[o], gall[:, 512:640])[0:KC]
            cbuf[at, C5:USED] = (
                mm(sct[o, 0:120], gall[:, 640:768])
                + mm(scy[o], gall[:, 768:896])
                + mm(scz[o], gall[:, 896:1024])
            )

    def rs_copy(t, way, sub):
        first, count = BACK[sub]
        return pltpu.make_async_remote_copy(
            src_ref=rsend.at[way, t, pl.ds(first, count)],
            dst_ref=rrecv.at[way, t, pl.ds(first, count)],
            send_sem=rs_ss.at[way, t, sub], recv_sem=rs_rs.at[way, t, sub],
            device_id={"dp": sides[way]}, device_id_type=MESH,
        )

    def rs_send(t, way, sub, at, add):
        first, count = BACK[sub]
        value = cbuf[at, first : first + count]
        if add:
            rs_copy(t - 1, way, sub).wait_recv()
            value = value + rrecv[way, t - 1, first : first + count].astype(F32)
        rsend[way, t, first : first + count] = value.astype(BF16)
        rs_copy(t, way, sub).start()

    def rs_sent(t):
        for sub in range(N):
            for way in range(2):
                if t > 0 or far(way, sub):
                    rs_copy(t, way, sub).wait_send()

    def owner(t, way):
        return lax.rem(z + 8 - t + Z, Z) if way == 0 else lax.rem(z + 8 + t, Z)

    def turn(part, subs):
        opposite = lax.rem(z + 8, Z)
        for sub in subs:
            ag_recv(7, 0 if far(0, sub) else 1, sub).wait_recv()
        forward(opposite, part)
        activate(part)
        term(opposite, part, 0)
        for sub in subs:
            rs_send(0, 0 if far(0, sub) else 1, sub, 0, False)
        for way in range(2):
            if any(not far(way, sub) for sub in subs):
                if part == 1:
                    term(owner(1, way), 0, 1)
                term(owner(1, way), part, 1)
                for sub in subs:
                    if not far(way, sub):
                        rs_send(1, way, sub, 1, False)

    turn(0, (0,))
    turn(1, (1,))
    turn(2, (2, 3))

    def back(low, high):
        for o in range(low, high):
            pairs = jnp.concatenate(
                [wbuf[o, first : first + KC] for first in range(0, C5, KC)], axis=1
            )
            block = wbuf[o, C5:USED]
            at = KC * o
            d32[at : at + KC, :] = mm_nt(pairs, gall[:, 0:640])
            d32[at : at + 120, :] = d32[at : at + 120, :] + mm_nt(block, gall[:, 640:768])
            low_rows = mm_nt(block, gall[:, 768:896])
            high_rows = mm_nt(block, gall[:, 896:1024])
            d32[at + 120 : at + 180, :] = (
                d32[at + 120 : at + 180, :] + low_rows[0:60] + high_rows[60:120]
            )

    def unscale():
        for first, count in THIRDS:
            bthird[first : first + count, :] = (
                d32[first : first + count, :] / fcol[first : first + count, 0:1]
            ).astype(BF16)
        bthird[D : 3 * WIDE, :] = jnp.zeros((3 * WIDE - D, ROWS), BF16)

    def expand(half):
        first = half * (E // 2) * BLK
        total = None
        for t in range(3):
            place = place_rows(t, True, first, (E // 2) * BLK)
            rows = mm_nt(place, bthird[WIDE * t : WIDE * (t + 1), :])
            total = rows if total is None else total + rows
        at = half * (E // 2)
        psend[at : at + E // 2] = total.astype(BF16).reshape(E // 2, BLK, WIDE)

    def p_copy(peer, block, slot_at, peer_sem):
        return pltpu.make_async_remote_copy(
            src_ref=psend.at[block], dst_ref=precv.at[slot_at],
            send_sem=p_ss.at[peer], recv_sem=p_rs.at[peer_sem],
            device_id={"ep": peer}, device_id_type=MESH,
        )

    def p_start():
        @pl.loop(1, E)
        def _(k):
            peer = lax.rem(me + k, E)
            p_copy(peer, peer, me, me).start()

        precv[me] = psend[me]

    def p_sent():
        @pl.loop(1, E)
        def _(k):
            peer = lax.rem(me + k, E)
            p_copy(peer, peer, me, me).wait_send()

    def p_wait():
        @pl.loop(1, E)
        def _(k):
            peer = lax.rem(me + E - k, E)
            p_copy(peer, 0, peer, peer).wait_recv()

    def combine(t):
        first, count = THIRDS[t]
        flat = precv[...].reshape(E * BLK, WIDE)
        pick = match_rows(E * BLK, 7)[t]
        dtok_ref[first : first + count, :] = mm_tn(flat[:, 0:count], pick).astype(BF16)

    rs_tasks = {
        (1, 0): lambda: back(0, 2),
        (1, 1): lambda: back(2, 4),
        (1, 2): lambda: back(4, 6),
        (1, 3): lambda: back(6, 8),
        (2, 0): lambda: back(8, 10),
        (2, 1): lambda: back(10, 12),
        (2, 2): lambda: back(12, 14),
        (2, 3): lambda: back(14, 16),
        (3, 0): unscale,
        (3, 1): lambda: expand(0),
        (3, 2): lambda: expand(1),
        (3, 3): p_start,
        (6, 1): lambda: (p_wait(), combine(0)),
        (6, 2): lambda: combine(1),
        (6, 3): lambda: combine(2),
        (7, 0): p_sent,
    }
    for t in range(1, 8):
        for sub in range(N):
            for way in range(2):
                if t == 1 and not far(way, sub):
                    continue
                if t == 1 and sub == 1:
                    term(owner(t, way), 0, way)
                if sub < 3:
                    term(owner(t, way), sub, way)
                elif t == 1:
                    term(owner(t, way), 2, way)
                rs_send(t, way, sub, way, True)
            rs_tasks.get((t, sub), lambda: None)()
        if t < 3:
            ag_sent(5 + t)
        else:
            rs_sent(t - 3)
    for sub in range(N):
        first, count = BACK[sub]
        if sub < 3:
            term(z, sub, 0)
        value = cbuf[0, first : first + count]
        for way in range(2):
            rs_copy(7, way, sub).wait_recv()
            value = value + rrecv[way, 7, first : first + count].astype(F32)
        cbuf[1, first : first + count] = value
        if sub == 1:
            for u in range(2):
                for half in range(2):
                    at = half * 2 * KC + u * KC
                    dw_ref[u, 0:KC, 128 * half : 128 * half + 128] = cbuf[1, at : at + KC]
    mixed = cbuf[1, C4:C5]
    dw_ref[0, 0:KC, 256:384] = mixed
    dw_ref[1, 0:KC, 256:384] = jnp.where(lanes(KC, 0, 24), roll(mixed, 24), 0.0)
    dw_ref[1, 0:120, 256:384] = jnp.where(
        lanes(120, 24, 104), roll(cbuf[1, C5:USED], 24), dw_ref[1, 0:120, 256:384]
    )
    low = jnp.where(lanes(60, 24, 72), roll(cbuf[1, C5 : C5 + 60], 72), 0.0)
    high = jnp.where(lanes(60, 72, 104), roll(cbuf[1, C5 + 60 : USED], 120), 0.0)
    dw_ref[1, 120:180, 256:384] = dw_ref[1, 120:180, 256:384] + low + high

    for t in range(5, 8):
        rs_sent(t)


def on_device(tokens, expert_ids, slot_pos, smooth, smoothed_weight, act_grad):
    w = jnp.transpose(smoothed_weight, (1, 0, 2))
    w = jnp.pad(w, ((0, 0), (0, KP - KC), (0, HP - HID)))
    vmem = pl.BlockSpec(memory_space=pltpu.VMEM)
    dw, dtok = pl.pallas_call(
        kernel,
        out_shape=(
            jax.ShapeDtypeStruct((2, KP, HP), F32),
            jax.ShapeDtypeStruct((D, 128), BF16),
        ),
        in_specs=[vmem, pl.BlockSpec(memory_space=pl.ANY)] + [vmem] * 4,
        out_specs=(vmem, vmem),
        scratch_shapes=[
            pltpu.VMEM((D, 128), BF16),
            pltpu.SemaphoreType.DMA,
            pltpu.VMEM((Z, CH, 128), BF16),
            pltpu.VMEM((4, BLK, WIDE), BF16),
            pltpu.VMEM((E, BLK, WIDE), BF16),
            pltpu.VMEM((4 * BLK, WIDE), F32),
            pltpu.VMEM((D + 64, ROWS), F32),
            pltpu.VMEM((Z, KP, ROWS), BF16),
            pltpu.VMEM((Z, 120, ROWS), BF16),
            pltpu.VMEM((Z, 120, ROWS), BF16),
            pltpu.VMEM((D, 8), F32),
            pltpu.VMEM((ROWS, 1024), F32),
            pltpu.VMEM((ROWS, 1024), BF16),
            pltpu.VMEM((2, CH, 128), F32),
            pltpu.VMEM((2, 8, CH, 128), BF16),
            pltpu.VMEM((2, 8, CH, 128), BF16),
            pltpu.VMEM((3 * WIDE, ROWS), BF16),
            pltpu.VMEM((E, BLK, WIDE), BF16),
            pltpu.VMEM((E, BLK, WIDE), BF16),
            pltpu.VMEM((ROWS, 128), F32),
            pltpu.SemaphoreType.DMA((2, 8, N)),
            pltpu.SemaphoreType.DMA((2, 8, N)),
            pltpu.SemaphoreType.DMA((2, 8, N)),
            pltpu.SemaphoreType.DMA((2, 8, N)),
            pltpu.SemaphoreType.DMA((E,)),
            pltpu.SemaphoreType.DMA((E,)),
            pltpu.SemaphoreType.DMA((E,)),
            pltpu.SemaphoreType.DMA((E,)),
        ],
        compiler_params=pltpu.CompilerParams(
            collective_id=0, has_side_effects=True, vmem_limit_bytes=48 * 1024 * 1024
        ),
    )(w, tokens[0].T, expert_ids[0].T, slot_pos[0].T, smooth, act_grad[0])
    dw = dw[:, :KC, :HID].transpose(1, 0, 2)
    return dtok.T[None], dw


def solution(mesh):
    return jax.shard_map(
        on_device,
        mesh=mesh,
        in_specs=(
            P("dp", "ep", None),
            P("dp", "ep", None),
            P("dp", "ep", None),
            P(),
            P("dp", None, "ep"),
            P("dp", None, "ep"),
        ),
        out_specs=(P("dp", "ep", None), P("dp", None, "ep")),
        check_vma=False,
    )
```

profile of v0, /device:TPU:8, one launch (start us, length us, event | category | flops | bytes accessed | tf_op | source)
XLA Modules:
  0.0 110.1 jit_solution(8556384295389317197)
XLA Ops:
  0.6 0.0 copy-start
  0.6 1.1 copy.11
  1.7 0.0 copy-start.1
  1.7 0.0 copy-start.2
  1.8 0.0 copy-start.4
  1.8 0.0 copy-start.3
  1.8 0.0 copy-done
  1.8 0.8 copy-done.1
  2.6 0.0 copy-done.2
  2.6 0.0 copy-done.4
  2.6 0.0 copy-done.3
  2.6 105.4 %shard_map.77 = (f32[2,184,384]{2,1,0:T(8,128)S(1)}, bf16[2880,128]{1,0:T(8,128)(2,1)S(1)}) custom-call(bf16[2,184,384]{2,1,0:T(8,128)(2,1)S(1)} %pad.4.w_ref, bf16[2880,128]{1,0:T(8,128)(2,1)S(1)} %bitcast.18, s32[4,128]{1,0:T(4,128)S(1)} %bitcast.21, s32[4,128]{1,0:T(4,128)S(1)} %bitcast.22, f32[4,2880]{1,0:T(4,128)S(1)} %copy-done.2, ...), custom_call_target="tpu_custom_call" | custom-call | tf_op jit(solution)/shard_map/pallas_call | solution.py:494
  108.1 1.1 copy.9
  109.2 0.9 copy.13
  (2 shorter events, 0.1 us)
Async XLA Ops:
  0.6 1.2 %copy-start = (bf16[1,128,2880]{1,2,0:T(8,128)(2,1)S(1)}, bf16[1,128,2880]{1,2,0:T(8,128)(2,1)}, u32[]{:S(2)}) copy-start(bf16[1,128,2880]{1,2,0:T(8,128)(2,1)} %param.6) | copy-start | bytes 2211844
  1.7 0.9 copy-start.1
  1.7 0.9 copy-start.2
  1.8 0.9 copy-start.4
  1.8 0.9 copy-start.3
where the time goes:
time: 110 us
  Pallas kernels  105 us (95%)
  local copies, waits for them, and re-layouts  3.95 us (4%)
    pallas_call x1, Pallas kernels, on_device(): pl.pallas_call(kernel, out_shape=(jax.ShapeDtypeStruct((2, KP, HP), F32),...  105 us
    unnamed x13, local copies, waits for them, and re-layouts  3.88 us

commit v1 on v0

--- a/solution.py
+++ b/solution.py
@@ -310,6 +310,9 @@
                 + mm(scz[o], gall[:, 896:1024])
             )
 
+    def edge(o, at):
+        cbuf[at, 340:360] = mm(sct[o, 160:KC], gall[:, 128:256])
+
     def rs_copy(t, way, sub):
         first, count = BACK[sub]
         return pltpu.make_async_remote_copy(
@@ -349,7 +352,7 @@
         for way in range(2):
             if any(not far(way, sub) for sub in subs):
                 if part == 1:
-                    term(owner(1, way), 0, 1)
+                    edge(owner(1, way), 1)
                 term(owner(1, way), part, 1)
                 for sub in subs:
                     if not far(way, sub):
@@ -448,7 +451,7 @@
                 if t == 1 and not far(way, sub):
                     continue
                 if t == 1 and sub == 1:
-                    term(owner(t, way), 0, way)
+                    edge(owner(t, way), way)
                 if sub < 3:
                     term(owner(t, way), sub, way)
                 elif t == 1:

time: 110 us -> 110 us (level)
  no operation moved by 1% of the time
where the time goes in v1:
time: 110 us
  Pallas kernels  105 us (95%)
  local copies, waits for them, and re-layouts  3.95 us (4%)
    pallas_call x1, Pallas kernels, on_device(): pl.pallas_call(kernel, out_shape=(jax.ShapeDtypeStruct((2, KP, HP), F32),...  105 us
    unnamed x13, local copies, waits for them, and re-layouts  3.88 us

profile of v1, /device:TPU:8, one launch (start us, length us, event | category | flops | bytes accessed | tf_op | source)
XLA Modules:
  0.0 110.1 jit_solution(12410088039242319158)
XLA Ops:
  0.6 0.0 copy-start
  0.6 1.1 copy.11
  1.7 0.0 copy-start.1
  1.7 0.0 copy-start.2
  1.8 0.0 copy-start.4
  1.8 0.0 copy-start.3
  1.8 0.0 copy-done
  1.8 0.8 copy-done.1
  2.6 0.0 copy-done.2
  2.6 0.0 copy-done.4
  2.6 0.0 copy-done.3
  2.6 105.4 %shard_map.77 = (f32[2,184,384]{2,1,0:T(8,128)S(1)}, bf16[2880,128]{1,0:T(8,128)(2,1)S(1)}) custom-call(bf16[2,184,384]{2,1,0:T(8,128)(2,1)S(1)} %pad.4.w_ref, bf16[2880,128]{1,0:T(8,128)(2,1)S(1)} %bitcast.18, s32[4,128]{1,0:T(4,128)S(1)} %bitcast.21, s32[4,128]{1,0:T(4,128)S(1)} %bitcast.22, f32[4,2880]{1,0:T(4,128)S(1)} %copy-done.2, ...), custom_call_target="tpu_custom_call" | custom-call | tf_op jit(solution)/shard_map/pallas_call | solution.py:497
  108.1 1.1 copy.9
  109.2 0.9 copy.13
  (2 shorter events, 0.1 us)
Async XLA Ops:
  0.6 1.2 %copy-start = (bf16[1,128,2880]{1,2,0:T(8,128)(2,1)S(1)}, bf16[1,128,2880]{1,2,0:T(8,128)(2,1)}, u32[]{:S(2)}) copy-start(bf16[1,128,2880]{1,2,0:T(8,128)(2,1)} %param.6) | copy-start | bytes 2211844
  1.7 0.9 copy-start.1
  1.7 0.9 copy-start.2
  1.8 0.9 copy-start.4
  1.8 0.9 copy-start.3
